TPU v7x, 1024 devices: a whole 4x8x16 slice. The times are simulated.
1024 devices in a mesh: row: 128 (over z_lo, y, core), rep: 8 (over z_hi, x).
Axes of the slice: x: 4, y: 8, z: 16 (z_hi: 2, z_lo: 8; z = z_hi * 8 + z_lo), core: 2. Of those that a mesh axis runs over, the one named last changes fastest.
Arguments:
- features: bfloat16 [262144, 128], P('row'), may hold values from -6 to 6
- weight: bfloat16 [128, 256], replicated, may hold values from -0.5 to 0.5
- section_source: int32 [16], P('rep'), may hold values from 0 to 127, as said below
- tile_columns: int32 [16, 2048, 3], P('rep', 'row'), may hold values from 0 to 15, as said below
- tile_counts: int32 [16, 2048], P('rep', 'row'), may hold values from 1 to 3
- tile_values: bfloat16 [16, 2048, 3, 128, 128], P('rep', 'row'), may hold values from 0.001876831 to 0.037353516
- cotangent: bfloat16 [262144, 256], P('row'), may hold values from -0.01171875 to 0.01171875
Outputs:
- activations: bfloat16 [262144, 256], P(('row', 'rep'))
- weight_grad: float32 [128, 256], replicated
Inputs may be any that keep to these rules, and one draw needn't show every extreme that they name: `section_source`: the 16 entries are distinct row groups. `tile_columns`: within one section and node block, the 3 slots name distinct blocks; slots from tile_counts on are ignored.
All inputs are finite; a program needn't handle non-finite values.
Results may differ from a plain program's by a relative error of at most 0.0053.
Values may be sent and summed in bfloat16 or wider, within the bound.
A program may use at most 32 MiB of HBM per device.

v0:
```python
import jax
import jax.numpy as jnp
from jax import lax
from jax.sharding import PartitionSpec as P


def broadcast(block, axis, source):
    block = jnp.where(lax.axis_index(axis) == source, block, jnp.zeros_like(block))
    return lax.psum(block, axis)


def body(features, weight, section_source, tile_columns, tile_counts, tile_values, cotangent):
    group_rows, width_in = features.shape
    group_count = tile_counts.shape[1]
    tile_edge = tile_values.shape[-1]
    slot_count = tile_values.shape[2]
    section_count = section_source.shape[0]
    slot_index = lax.broadcasted_iota(jnp.int32, (group_count, slot_count), 1)
    summed = jnp.zeros((group_count, tile_edge, width_in), jnp.float32)
    for section_step in range(section_count):
        root_group = section_source[section_step]
        source = broadcast(features, "row", root_group)
        source_blocks = source.reshape(group_count, tile_edge, width_in)
        picked = jnp.take(source_blocks, tile_columns[section_step], axis=0)
        live_slot = slot_index < tile_counts[section_step][:, None]
        tile_data = jnp.where(
            live_slot[:, :, None, None], tile_values[section_step], jnp.zeros((), jnp.bfloat16)
        )
        summed = summed + jnp.einsum(
            "bmij,bmjf->bif", tile_data, picked, preferred_element_type=jnp.float32
        )
    summed = summed.reshape(group_rows, width_in)
    own_rows = lax.psum_scatter(summed, "rep", scatter_dimension=0, tiled=True)
    aggregate = own_rows.astype(jnp.bfloat16)
    row_count = aggregate.shape[0]
    first_row = lax.axis_index("rep") * row_count
    grad_rows = lax.dynamic_slice_in_dim(cotangent, first_row, row_count, 0)
    preact = jnp.dot(aggregate, weight, preferred_element_type=jnp.float32)
    sigmoid_v = jax.nn.sigmoid(preact)
    activations = (preact * sigmoid_v).astype(jnp.bfloat16)
    slope_v = sigmoid_v * (1.0 + preact * (1.0 - sigmoid_v))
    pre_grad = (grad_rows.astype(jnp.float32) * slope_v).astype(jnp.bfloat16)
    partial_grad = lax.dot_general(
        aggregate, pre_grad, (((0,), (0,)), ((), ())), preferred_element_type=jnp.float32
    )
    weight_grad = lax.psum(partial_grad, ("row", "rep"))
    return (activations, weight_grad)


def solution(mesh):
    in_specs = (
        P("row", None),
        P(),
        P("rep"),
        P("rep", "row", None),
        P("rep", "row"),
        P("rep", "row", None, None, None),
        P("row", None),
    )
    out_specs = (P(("row", "rep"), None), P())
    return jax.shard_map(body, mesh=mesh, in_specs=in_specs, out_specs=out_specs, check_vma=False)
```

profile of v0, /device:TPU:1, one launch (start us, length us, event | category | flops | bytes accessed | tf_op | source)
XLA Modules:
  0.0 2254.2 jit_solution(17143979695928869730)
XLA Ops:
  7.2 0.0 copy-start
  7.2 0.0 copy-start.3
  7.2 0.0 copy-start.4
  7.2 0.0 all-reduce.6.cloned.1.call-start
  7.3 1.3 fusion.34
  9.9 2.1 broadcast_select_fusion
  12.0 0.0 all-reduce.6.cloned.1.call-update
  12.0 0.0 reduce-scatter.2.cloned.1.call-start
  12.1 0.0 copy-done.3
  12.1 0.1 copy.14
  12.2 0.1 reshape.85
  12.3 0.1 copy.13
  12.4 0.1 copy.16
  12.5 0.1 reshape.89
  12.5 0.1 copy.15
  12.7 0.0 copy-done.4
  12.7 0.1 iota_compare_fusion.1
  12.8 0.1 iota_compare_fusion
  12.8 1640.4 %all-reduce.6.cloned.1.call-done = (bf16[16,128,128]{2,1,0:T(8,128)(2,1)}, bf16[16,128,128]{2,1,0:T(8,128)(2,1)}) async-done(((bf16[16,128,128]{2,1,0:T(8,128)(2,1)}, bf16[16,128,128]{2,1,0:T(8,128)(2,1)}), (bf16[16,128,128]{2,1,0:T(8,128)(2,1)}, bf16[16,128,128]{2,1,0:T(8,128)(2,1)})) %all-reduce.6.cloned.1.call-update) | async-done | bytes 1048592 | tf_op jit(solution)/shard_map/psum | solution.py:9
  1653.3 0.0 copy-start.1
  1653.3 1.9 gather_fusion
  1655.2 0.0 copy-done.1
  1655.3 2.0 gather_fusion.1
  1657.2 0.0 copy-start.2
  1657.2 0.0 copy-start.5
  1657.2 2.2 fusion.10
  1659.5 0.0 copy-done.2
  1659.5 0.6 copy-done.5
  1660.1 1.6 fusion.16
  1661.7 0.0 reduce-scatter.2.cloned.1.call-update
  1661.7 0.0 all-reduce.4.cloned.1.call-start
  1661.8 121.6 %reduce-scatter.2.cloned.1.call-done = f32[256,128]{1,0:T(8,128)} async-done(((f32[2048,128]{1,0:T(8,128)}), f32[256,128]{1,0:T(8,128)}) %reduce-scatter.2.cloned.1.call-update) | async-done | bytes 131088 | tf_op jit(solution)/shard_map/reduce_scatter | solution.py:33
  1783.3 0.0 copy-done
  1783.3 1.8 multiply_convert_fusion.1
  1785.1 1.9 fusion.23
  1787.0 0.0 all-reduce.4.cloned.1.call-update
  1787.0 459.1 %all-reduce.4.cloned.1.call-done = f32[128,256]{1,0:T(8,128)} async-done(((f32[128,256]{1,0:T(8,128)}), f32[128,256]{1,0:T(8,128)}) %all-reduce.4.cloned.1.call-update) | async-done | bytes 131088 | tf_op jit(solution)/shard_map/psum | solution.py:46
  2246.1 1.6 copy.30
  (6 shorter events, 0.0 us)
Async XLA Ops:
  7.2 1776.2 %copy-start = (bf16[128,256]{1,0:T(8,128)(2,1)S(1)}, bf16[128,256]{1,0:T(8,128)(2,1)}, u32[]{:S(2)}) copy-start(bf16[128,256]{1,0:T(8,128)(2,1)} %param.10) | copy-start | bytes 196612
  7.2 4.9 copy-start.3
  7.2 5.5 copy-start.4
  7.2 1646.1 %all-reduce.6.cloned.1.call-start = ((), (), s32[]{:S(2)}) async-start(), calls=%async_computation.3 | async-start | bytes 2097152 | tf_op jit(solution)/shard_map/psum | solution.py:9
  12.0 1771.3 %reduce-scatter.2.cloned.1.call-start = ((), (), s32[]{:S(2)}) async-start(), calls=%async_computation.1 | async-start | bytes 1179648 | tf_op jit(solution)/shard_map/reduce_scatter | solution.py:33
  1653.3 2.0 copy-start.1
  1657.2 2.2 copy-start.2
  1657.2 2.8 copy-start.5
  1661.7 584.4 %all-reduce.4.cloned.1.call-start = ((), (), s32[]{:S(2)}) async-start(), calls=%async_computation.2 | async-start | bytes 262144 | tf_op jit(solution)/shard_map/psum | solution.py:46
Sparse Core Ops, SparseCore 0:
  12.1 1641.1 all-reduce.5
  1661.9 121.4 reduce-scatter.1
  1789.4 456.6 all-reduce.3
where the time goes:
time: 2250 us
  waiting for transfers between devices  2220 us (99%)
    psum x1, waiting for transfers between devices, broadcast(): return lax.psum(block, axis)  1640 us
    psum x1, waiting for transfers between devices, body(): weight_grad = lax.psum(partial_grad, ('row', 'rep'))  459 us
    reduce_scatter x1, waiting for transfers between devices, body(): own_rows = lax.psum_scatter(summed, 'rep', scatter_dimension=0, tiled=True)  122 us
  transfers between devices with their start and end apart: 3, of which 3 were waited for; matrix products, arithmetic and copies ran while one was open for 0% of the time, Pallas kernels for 0%

commit v1 on v0

v1 whole, which is shorter than its diff:
```python
import functools

import jax
import jax.numpy as jnp
from jax import lax
from jax.experimental import pallas as pl
from jax.experimental.pallas import tpu as pltpu
from jax.sharding import PartitionSpec as P

MESH = pl.DeviceIdType.MESH
BF16, F32 = jnp.bfloat16, jnp.float32

NZ, NY, NC, NH, NX = 8, 8, 2, 2, 4
ROW_SUM = F32
HALF_SUM = F32
GRAD_A = BF16
GRAD_B = F32


def remote(src, dst, sems, slot, row, rep):
    send, recv = sems
    return pltpu.make_async_remote_copy(
        src_ref=src,
        dst_ref=dst,
        send_sem=send.at[slot],
        recv_sem=recv.at[slot],
        device_id={"row": row, "rep": rep},
        device_id_type=MESH,
    )


def kernel(
    source_ref,
    column_ref,
    count_ref,
    weight_ref,
    features_ref,
    tiles_ref,
    cotangent_ref,
    act_ref,
    grad_ref,
    tiles,
    cot,
    ids,
    cand,
    pick,
    pieces,
    zcand,
    gathered,
    agg,
    xsum,
    own,
    zsum,
    zsend,
    wsend,
    wrecv,
    xgrad,
    zgrad,
    wfull,
    local_sem,
    *sems,
):
    nq = NY * NC
    section_count, block_count, slot_count = tiles.shape[:3]
    sa, si, sx, sr, sg, sy, sc, sp, sh, sw, sv, su, so = [
        (sems[2 * i], sems[2 * i + 1]) for i in range(13)
    ]
    row, rep = lax.axis_index("row"), lax.axis_index("rep")
    zl, q = row // nq, row % nq
    y, c = q // NC, q % NC
    zh, x = rep // NX, rep % NX
    z = zh * NZ + zl

    def q_at(d):
        dy, dc = d // NC, d % NC
        return ((y + dy) % NY) * NC + (c + dc) % NC

    def row_q(d):
        return zl * nq + q_at(d)

    def rep_x(d):
        return zh * NX + (x + d) % NX

    def zlo_at(d):
        return (zl + d) % NZ

    def z_pos(d):
        return (z + d) % (NZ * NH)

    def z_dev(d):
        zz = z_pos(d)
        return (zz % NZ) * nq + q, (zz // NZ) * NX + x

    tile_copy = pltpu.make_async_copy(tiles_ref, tiles, local_sem.at[0])
    tile_copy.start()
    own_rows = cot.shape[0]
    cot_copy = pltpu.make_async_copy(
        cotangent_ref.at[pl.ds(pl.multiple_of(rep * own_rows, own_rows), own_rows)],
        cot,
        local_sem.at[1],
    )
    cot_copy.start()

    barrier = pltpu.get_barrier_semaphore()
    peers = [(row_q(d), rep) for d in range(1, nq)]
    peers += [(row, rep_x(d)) for d in range(1, NX)]
    peers += [z_dev(d) for d in range(1, NZ * NH)]
    for r, p in peers:
        pl.semaphore_signal(
            barrier, inc=1, device_id={"row": r, "rep": p}, device_id_type=MESH
        )

    for k in range(section_count):
        ids[x, k] = jnp.full(ids.shape[2:], (source_ref[k] % nq).astype(F32)).astype(BF16)
    gathered[:, block_count] = jnp.zeros(
        (section_count,) + gathered.shape[2:], BF16
    )

    pl.semaphore_wait(barrier, len(peers))

    pending = []

    per_x = NZ // NX

    def rows_for(dq):
        return features_ref.at[pl.ds(dq * NZ + x * per_x, per_x)]

    id_copies = []
    for d in range(1, NX):
        copy = remote(ids.at[x], ids.at[x], si, d, row, rep_x(d))
        copy.start()
        id_copies.append(copy)
    a_copies = []
    for d in range(1, nq):
        copy = remote(rows_for(q_at(d)), cand.at[q], sa, d, row_q(d), rep)
        copy.start()
        a_copies.append(copy)
    own_copy = pltpu.make_async_copy(rows_for(q), cand.at[q], local_sem.at[2])
    own_copy.start()
    own_copy.wait()
    for copy in id_copies + a_copies:
        copy.wait_recv()
    pending += id_copies + a_copies

    x_copies = []
    for d in list(range(1, NX)) + [0]:
        tx = (x + d) % NX
        for k in range(section_count):
            want = ids[tx, k][None]
            chosen = cand[0]
            for s in range(1, nq):
                chosen = jnp.where(want == jnp.asarray(s, BF16), cand[s], chosen)
            if d == 0:
                pieces[k, pl.ds(x * per_x, per_x)] = chosen
            else:
                pick[d, k] = chosen
        if d != 0:
            copy = remote(
                pick.at[d], pieces.at[:, pl.ds(x * per_x, per_x)], sx, d, row, rep_x(d)
            )
            copy.start()
            x_copies.append(copy)
    for copy in x_copies:
        copy.wait_recv()
    pending += x_copies

    r_copies = []
    for d in range(1, NZ):
        t = zlo_at(d)
        copy = remote(pieces.at[:, t], zcand.at[zl], sr, d, t * nq + q, rep)
        copy.start()
        r_copies.append(copy)
    zcand[zl] = pieces[:, zl]
    for copy in r_copies:
        copy.wait_recv()
    pending += r_copies
    for k in range(section_count):
        gathered[k, q, zl] = zcand[source_ref[k] // nq, k]

    g_copies = []
    for d in range(1, NZ):
        t = zlo_at(d)
        mine = gathered.at[:, q, zl]
        copy = remote(mine, mine, sg, d, t * nq + q, rep)
        copy.start()
        g_copies.append(copy)
    for copy in g_copies:
        copy.wait_recv()
    pending += g_copies

    block = gathered.at[:, q]
    sib_row = row_q(1) if NC == 2 else row
    y_copies = []
    for dy in range(1, NY):
        copy = remote(block, block, sy, dy, row_q(dy * NC), rep)
        copy.start()
        y_copies.append(copy)
    c_copies = []
    for dy in range(NY):
        if dy > 0:
            y_copies[dy - 1].wait_recv()
        got = gathered.at[:, q_at(((NY - dy) % NY) * NC)]
        copy = remote(got, got, sc, dy, sib_row, rep)
        copy.start()
        c_copies.append(copy)
    for copy in c_copies:
        copy.wait_recv()
    pending += y_copies + c_copies

    tile_copy.wait()
    per_owner = block_count // (NH * NX)
    edge = agg.shape[-1]

    def product(b):
        left, right = [], []
        for k in range(section_count):
            for m in range(slot_count):
                live = m < count_ref[k, b]
                col = jnp.where(live, column_ref[k, b, m], block_count)
                left.append(tiles[k, b, m])
                right.append(gathered[k, col].reshape(edge, edge))
        return jnp.dot(
            jnp.concatenate(left, axis=1),
            jnp.concatenate(right, axis=0),
            preferred_element_type=F32,
        )

    p_copies = []
    for d in list(range(1, NX)) + [0]:
        tx = (x + d) % NX
        for h in range(NH):
            def one(j, _, tx=tx, h=h):
                value = product((h * NX + tx) * per_owner + j)
                if d == 0:
                    own[h, j] = value
                else:
                    agg[d, h, j] = value.astype(ROW_SUM)
                return _

            lax.fori_loop(0, per_owner, one, 0)
        if d != 0:
            copy = remote(agg.at[d], xsum.at[d], sp, d, row, rep_x(d))
            copy.start()
            p_copies.append(copy)
    for copy in p_copies:
        copy.wait_recv()
    pending += p_copies

    def total(h):
        out = own[h]
        for d in range(1, NX):
            out = out + xsum[d, h].astype(F32)
        return out

    if NH == 2:
        zsend[...] = total(1 - zh).astype(HALF_SUM)
        partner = z_dev(NZ)
        h_copy = remote(zsend, zsum, sh, 0, partner[0], partner[1])
        h_copy.start()
        kept = total(zh)
        h_copy.wait_recv()
        pending.append(h_copy)
        summed = kept + zsum[...].astype(F32)
    else:
        summed = total(0)
    aggregate = summed.reshape(own_rows, edge).astype(BF16)

    preact = jnp.dot(aggregate, weight_ref[...], preferred_element_type=F32)
    sigmoid = jax.nn.sigmoid(preact)
    act_ref[...] = (preact * sigmoid).astype(BF16)
    slope = sigmoid * (1.0 + preact * (1.0 - sigmoid))
    cot_copy.wait()
    pre_grad = (cot[...].astype(F32) * slope).astype(BF16)
    part = lax.dot_general(
        aggregate, pre_grad, (((0,), (0,)), ((), ())), preferred_element_type=F32
    )
    tall, wide = wsend.shape[1:]
    across = part.shape[1] // wide
    for t in range(nq):
        top, left = (t // across) * tall, (t % across) * wide
        wsend[t] = part[top : top + tall, left : left + wide].astype(GRAD_A)

    w_copies = []
    for d in range(1, nq):
        copy = remote(wsend.at[q_at(d)], wrecv.at[q], sw, d, row_q(d), rep)
        copy.start()
        w_copies.append(copy)
    wrecv[q] = wsend[q]
    for copy in w_copies:
        copy.wait_recv()
    pending += w_copies
    xgrad[x] = functools.reduce(
        lambda a, b: a + b, [wrecv[t].astype(F32) for t in range(nq)]
    ).astype(GRAD_B)
    v_copies = []
    for d in range(1, NX):
        copy = remote(xgrad.at[x], xgrad.at[x], sv, d, row, rep_x(d))
        copy.start()
        v_copies.append(copy)
    for copy in v_copies:
        copy.wait_recv()
    pending += v_copies
    zgrad[z] = functools.reduce(
        lambda a, b: a + b, [xgrad[t].astype(F32) for t in range(NX)]
    ).astype(GRAD_B)
    u_copies = []
    for d in range(1, NZ * NH):
        r, p = z_dev(d)
        copy = remote(zgrad.at[z], zgrad.at[z], su, d, r, p)
        copy.start()
        u_copies.append(copy)
    for copy in u_copies:
        copy.wait_recv()
    pending += u_copies
    wfull[q] = functools.reduce(
        lambda a, b: a + b, [zgrad[t].astype(F32) for t in range(NZ * NH)]
    ).astype(GRAD_B)
    o_copies = []
    for d in range(1, nq):
        copy = remote(wfull.at[q], wfull.at[q], so, d, row_q(d), rep)
        copy.start()
        o_copies.append(copy)
    for copy in o_copies:
        copy.wait_recv()
    pending += o_copies
    for t in range(nq):
        top, left = (t // across) * tall, (t % across) * wide
        grad_ref[top : top + tall, left : left + wide] = wfull[t].astype(F32)

    for copy in pending:
        copy.wait_send()


def body(features, weight, section_source, tile_columns, tile_counts, tile_values, cotangent):
    rows, width = features.shape
    sections, blocks, slots, edge, _ = tile_values.shape
    hidden = weight.shape[1]
    nq = NY * NC
    piece = edge // NZ
    own_rows = rows // (NH * NX)
    per_owner = blocks // (NH * NX)
    per_x = NZ // NX
    tall = width * (hidden // edge) // nq
    dma = pltpu.SemaphoreType.DMA
    counts = [nq, NX, NX, NZ, NZ, NY, NY, NX, 1, nq, NX, NZ * NH, nq]
    smem = pl.BlockSpec(memory_space=pltpu.SMEM)
    vmem = pl.BlockSpec(memory_space=pltpu.VMEM)
    hbm = pl.BlockSpec(memory_space=pltpu.HBM)
    return pl.pallas_call(
        kernel,
        out_shape=(
            jax.ShapeDtypeStruct((own_rows, hidden), BF16),
            jax.ShapeDtypeStruct((width, hidden), F32),
        ),
        in_specs=[smem, smem, smem, vmem, hbm, hbm, hbm],
        out_specs=(vmem, vmem),
        scratch_shapes=[
            pltpu.VMEM(tile_values.shape, BF16),
            pltpu.VMEM((own_rows, hidden), BF16),
            pltpu.VMEM((NX, sections, piece, width), BF16),
            pltpu.VMEM((nq, per_x, piece, width), BF16),
            pltpu.VMEM((NX, sections, per_x, piece, width), BF16),
            pltpu.VMEM((sections, NZ, piece, width), BF16),
            pltpu.VMEM((NZ, sections, piece, width), BF16),
            pltpu.VMEM((sections, blocks + 1, NZ, piece, width), BF16),
            pltpu.VMEM((NX, NH, per_owner, edge, width), ROW_SUM),
            pltpu.VMEM((NX, NH, per_owner, edge, width), ROW_SUM),
            pltpu.VMEM((NH, per_owner, edge, width), F32),
            pltpu.VMEM((per_owner, edge, width), HALF_SUM),
            pltpu.VMEM((per_owner, edge, width), HALF_SUM),
            pltpu.VMEM((nq, tall, edge), GRAD_A),
            pltpu.VMEM((nq, tall, edge), GRAD_A),
            pltpu.VMEM((NX, tall, edge), GRAD_B),
            pltpu.VMEM((NZ * NH, tall, edge), GRAD_B),
            pltpu.VMEM((nq, tall, edge), GRAD_B),
            dma((3,)),
        ]
        + [dma((n,)) for n in counts for _ in range(2)],
        compiler_params=pltpu.CompilerParams(
            collective_id=0, has_side_effects=True, vmem_limit_bytes=48 * 1024 * 1024
        ),
        cost_estimate=pl.CostEstimate(
            flops=2 * sections * blocks * slots * edge * edge * width,
            bytes_accessed=tile_values.size * 2,
            transcendentals=own_rows * hidden,
        ),
    )(
        section_source,
        tile_columns,
        tile_counts,
        weight,
        features.reshape(rows // piece, piece, width),
        tile_values,
        cotangent,
    )


def solution(mesh):
    in_specs = (
        P("row", None),
        P(),
        P("rep"),
        P("rep", "row", None),
        P("rep", "row"),
        P("rep", "row", None, None, None),
        P("row", None),
    )
    out_specs = (P(("row", "rep"), None), P())
    return jax.shard_map(body, mesh=mesh, in_specs=in_specs, out_specs=out_specs, check_vma=False)
```

time: 2250 us -> 128 us (0.06)
  waiting for transfers between devices: 2220 us -> 0 us
  Pallas kernels: 0 us -> 118 us
    psum x2 -> x0, waiting for transfers between devices: 2100 us -> none  [the longest x1 1640 us: broadcast(): return lax.psum(block, axis)]
    reduce_scatter x1 -> x0, waiting for transfers between devices: 122 us -> none  [body(): own_rows = lax.psum_scatter(summed, 'rep', scatter_dimension=0, tiled=True)]
    pallas_call x0 -> x1, Pallas kernels: none -> 118 us  [body(): pl.pallas_call(kernel, out_shape=(jax.ShapeDtypeStruct((own_rows, hidden)...]
  transfers between devices with their start and end apart: 3 -> 0, of which waited for: 3 -> 0; matrix products, arithmetic and copies ran while one was open for 0% -> 0% of each run, Pallas kernels for 0% -> 0%
where the time goes in v1:
time: 128 us; the launch traced here: 127 us
  Pallas kernels  118 us (92%)
  local copies, waits for them, and re-layouts  8.41 us (7%)
    pallas_call x1, Pallas kernels, body(): pl.pallas_call(kernel, out_shape=(jax.ShapeDtypeStruct((own_rows, hidden)...  118 us
    unnamed x15, local copies, waits for them, and re-layouts  8.41 us

profile of v1, /device:TPU:1, one launch (start us, length us, event | category | flops | bytes accessed | tf_op | source)
XLA Modules:
  0.0 127.1 jit_solution(3083674262953993672)
XLA Ops:
  0.6 0.8 copy.9.column_ref
  1.4 0.0 copy-start
  1.4 1.9 %copy-done = bf16[2,16,3,128,128]{4,3,2,1,0:T(8,128)(2,1)S(1)} copy-done((bf16[2,16,3,128,128]{4,3,2,1,0:T(8,128)(2,1)S(1)}, bf16[2,16,3,128,128]{4,3,2,1,0:T(8,128)(2,1)}, u32[]{:S(2)}) %copy-start) | copy-done | bytes 3145752
  3.3 0.0 copy-start.1
  3.3 1.2 copy-done.1
  4.5 0.0 copy-start.2
  4.5 1.0 copy-done.2
  5.6 0.0 copy-start.3
  5.6 0.8 copy-done.3
  6.4 0.0 copy-start.4
  6.4 0.7 copy-done.4
  7.1 0.0 copy-start.5
  7.1 0.7 copy-done.5
  7.7 118.1 %shard_map.86 = (bf16[256,256]{1,0:T(8,128)(2,1)S(1)}, f32[128,256]{1,0:T(8,128)S(1)}) custom-call(s32[2]{0:T(128)S(1)} %copy-done.5, s32[2,16,3]{2,1,0:T(8,128)S(1)} %copy.9.column_ref, s32[2,16]{1,0:T(2,128)S(1)} %copy-done.4, bf16[128,256]{1,0:T(8,128)(2,1)S(1)} %copy-done.3, bf16[128,16,128]{2,1,0:T(8,128)(2,1)S(1)} %bitcast.1, ...), custom_call_target="tpu_custom_call" | custom-call | flops 402653184 | bytes 3145728 | tf_op jit(solution)/shard_map/pallas_call | solution.py:349
  125.8 0.7 copy.12
  126.5 0.7 copy.13
Async XLA Ops:
  1.4 1.9 %copy-start = (bf16[2,16,3,128,128]{4,3,2,1,0:T(8,128)(2,1)S(1)}, bf16[2,16,3,128,128]{4,3,2,1,0:T(8,128)(2,1)}, u32[]{:S(2)}) copy-start(bf16[2,16,3,128,128]{4,3,2,1,0:T(8,128)(2,1)} %tiles_ref.1) | copy-start | bytes 9437188
  3.3 1.2 copy-start.1
  4.5 1.0 copy-start.2
  5.6 0.8 copy-start.3
  6.4 0.7 copy-start.4
  7.1 0.7 copy-start.5

commit v2 on v1

v2 whole, which is shorter than its diff:
```python
import functools

import jax
import jax.numpy as jnp
from jax import lax
from jax.experimental import pallas as pl
from jax.experimental.pallas import tpu as pltpu
from jax.sharding import PartitionSpec as P

MESH = pl.DeviceIdType.MESH
BF16, F32 = jnp.bfloat16, jnp.float32

NZ, NY, NC, NH, NX = 8, 8, 2, 2, 4
ROW_SUM = BF16
HALF_SUM = BF16
GRAD_A = BF16
GRAD_B = F32


def remote(src, dst, sems, slot, row, rep):
    send, recv = sems
    return pltpu.make_async_remote_copy(
        src_ref=src,
        dst_ref=dst,
        send_sem=send.at[slot],
        recv_sem=recv.at[slot],
        device_id={"row": row, "rep": rep},
        device_id_type=MESH,
    )


def kernel(
    source_ref,
    column_ref,
    count_ref,
    weight_hbm,
    features_ref,
    tiles_ref,
    cotangent_ref,
    act_ref,
    grad_ref,
    tiles,
    cot,
    weight_ref,
    ids,
    cand,
    pick,
    pieces,
    zcand,
    held,
    gathered,
    agg,
    xsum,
    own,
    zsum,
    zsend,
    wsend,
    wrecv,
    xgrad,
    zgrad,
    wfull,
    local_sem,
    far_sem,
    *sems,
):
    nq = NY * NC
    section_count, block_count, slot_count = tiles.shape[:3]
    sa, si, sx, sr, sg, sy, sc, sp, sh, sw, sv, su, so = [
        (sems[2 * i], sems[2 * i + 1]) for i in range(13)
    ]
    row, rep = lax.axis_index("row"), lax.axis_index("rep")
    zl, q = row // nq, row % nq
    y, c = q // NC, q % NC
    zh, x = rep // NX, rep % NX
    z = zh * NZ + zl

    def q_at(d):
        dy, dc = d // NC, d % NC
        return ((y + dy) % NY) * NC + (c + dc) % NC

    def row_q(d):
        return zl * nq + q_at(d)

    def rep_x(d):
        return zh * NX + (x + d) % NX

    def z_pos(d):
        return (z + d + NZ * NH) % (NZ * NH)

    def z_dev(d):
        zz = z_pos(d)
        return (zz % NZ) * nq + q, (zz // NZ) * NX + x

    barrier = pltpu.get_barrier_semaphore()
    peers = [(row_q(d), rep) for d in range(1, nq)]
    peers += [(row, rep_x(d)) for d in range(1, NX)]
    half = NZ // 2
    close = [d for n in range(1, half + 1) for d in (-n, n)]
    peers += [z_dev(d) for d in close]
    over = (zl // half) * NZ - half
    over_row, over_rep = z_dev(over)
    over_h = over_rep // NX
    peers += [(over_row, over_h * NX + (x + d) % NX) for d in range(1, NX)]
    for r, p in peers:
        pl.semaphore_signal(
            barrier, inc=1, device_id={"row": r, "rep": p}, device_id_type=MESH
        )

    tile_copy = pltpu.make_async_copy(tiles_ref, tiles, local_sem.at[0])
    tile_copy.start()
    own_rows = cot.shape[0]
    cot_copy = pltpu.make_async_copy(
        cotangent_ref.at[pl.ds(pl.multiple_of(rep * own_rows, own_rows), own_rows)],
        cot,
        local_sem.at[1],
    )
    cot_copy.start()
    weight_copy = pltpu.make_async_copy(weight_hbm, weight_ref, local_sem.at[3])
    weight_copy.start()

    piece = ids.shape[2]
    share_rows = piece // section_count
    which = lax.broadcasted_iota(jnp.int32, ids.shape[2:], 0) // share_rows
    mixed = jnp.zeros(ids.shape[2:], jnp.int32)
    for k in range(section_count):
        mixed = jnp.where(which == k, source_ref[k], mixed)
    ids[zh, x] = mixed.astype(F32).astype(BF16)
    gathered[:, block_count] = jnp.zeros(
        (section_count,) + gathered.shape[2:], BF16
    )

    pl.semaphore_wait(barrier, len(peers))

    pending = []

    per_x = NZ // NX

    def rows_for(dq):
        return features_ref.at[pl.ds(dq * NZ + x * per_x, per_x)]

    own_ids = ids.at[zh, x]
    id_copies = []
    for d in range(NX):
        dest = over_h * NX + (x + d) % NX
        id_copies.append(remote(own_ids, own_ids, si, NX + d, over_row, dest))
    for d in range(1, NX):
        id_copies.append(remote(own_ids, own_ids, si, d, row, rep_x(d)))
    for copy in id_copies:
        copy.start()
    a_copies = []
    for d in range(1, nq):
        copy = remote(rows_for(q_at(d)), cand.at[q], sa, d, row_q(d), rep)
        copy.start()
        a_copies.append(copy)
    own_copy = pltpu.make_async_copy(rows_for(q), cand.at[q], local_sem.at[2])
    own_copy.start()
    for d in close:
        r, p = z_dev(d)
        pl.semaphore_signal(
            far_sem, inc=1, device_id={"row": r, "rep": p}, device_id_type=MESH
        )
    own_copy.wait()
    for copy in id_copies + a_copies:
        copy.wait_recv()
    pending += id_copies + a_copies

    def wanted(h, t, k):
        first = ids[h, t].astype(F32)[k * share_rows : k * share_rows + 1]
        full = jnp.broadcast_to(first, ids.shape[2:])
        group = jnp.floor(full * (1.0 / nq))
        return group.astype(BF16), (full - group * nq).astype(BF16)

    here = pl.ds(x * per_x, per_x)

    def give(d):
        return remote(
            pick.at[(x + d) % NX], pieces.at[:, :, here], sx, d, row, rep_x(d)
        )

    def choose(i, carry):
        d = (i + 1) % NX
        t = (x + d) % NX
        for h in range(NH):
            for k in range(section_count):
                want = wanted(h, t, k)[1][None]
                chosen = cand[0]
                for s in range(1, nq):
                    chosen = jnp.where(want == jnp.asarray(s, BF16), cand[s], chosen)
                pick[t, h, k] = chosen

        @pl.when(i < NX - 1)
        def _():
            give(d).start()

        return carry

    lax.fori_loop(0, NX, choose, 0)
    x_copies = [give(d) for d in range(1, NX)]
    pieces[:, :, here] = pick[x]
    for copy in x_copies:
        copy.wait_recv()
    pending += x_copies

    near = [d for n in range(half, 0, -1) for d in (-n, n) if d < half]
    r_copies = []
    for i, d in enumerate(near):
        r, p = z_dev(d)
        copy = remote(pieces.at[:, :, r // nq], zcand.at[zl], sr, i, r, p)
        copy.start()
        r_copies.append(copy)
    zcand[zl] = pieces[:, :, zl]
    for copy in r_copies:
        copy.wait_recv()
    pending += r_copies
    for h in range(NH):
        for k in range(section_count):
            want = wanted(h, x, k)[0]
            chosen = zcand[0, h, k]
            for s in range(1, NZ):
                chosen = jnp.where(want == jnp.asarray(s, BF16), zcand[s, h, k], chosen)
            held[h, k] = chosen

    g_copies = []
    for i, d in enumerate(near):
        r, p = z_dev(d)
        copy = remote(held.at[p // NX], gathered.at[:, q, zl], sg, i, r, p)
        copy.start()
        g_copies.append(copy)
    gathered[:, q, zl] = held[zh]
    for copy in g_copies:
        copy.wait_recv()
    pending += g_copies

    def y_step(dy):
        return q_at((dy % NY) * NC)

    def y_send(origin, dy, slot, only=None):
        ref = gathered.at[:, y_step(origin)]
        if only is not None:
            ref = gathered.at[only, y_step(origin)]
        copy = remote(ref, ref, sy, slot, zl * nq + y_step(dy), rep)
        copy.start()
        pending.append(copy)
        return copy

    c_copies = []

    def hand_on(dy):
        ref = gathered.at[:, y_step(dy)]
        copy = remote(ref, ref, sc, dy % NY, row_q(1), rep)
        copy.start()
        c_copies.append(copy)

    up2 = y_send(0, 2, 0)
    down2 = y_send(0, -2, 1)
    up1 = y_send(0, 1, 2)
    down1 = y_send(0, -1, 3)
    hand_on(0)
    up2.wait_recv()
    up4 = y_send(-2, 2, 4, 0)
    up3 = y_send(-2, 1, 5)
    hand_on(-2)
    down2.wait_recv()
    down4 = y_send(2, -2, 6, 1)
    down3 = y_send(2, -1, 7)
    hand_on(2)
    up1.wait_recv()
    hand_on(-1)
    down1.wait_recv()
    hand_on(1)
    up3.wait_recv()
    hand_on(-3)
    down3.wait_recv()
    hand_on(3)
    up4.wait_recv()
    down4.wait_recv()
    hand_on(4)
    for copy in c_copies:
        copy.wait_recv()
    pending += c_copies

    tile_copy.wait()
    per_owner = block_count // (NH * NX)
    edge = agg.shape[-1]

    def product(b):
        left, right = [], []
        for k in range(section_count):
            for m in range(slot_count):
                live = m < count_ref[k, b]
                col = jnp.where(live, column_ref[m, k, b], block_count)
                left.append(tiles[k, b, m])
                right.append(gathered[k, col].reshape(edge, edge))
        return jnp.dot(
            jnp.concatenate(left, axis=1),
            jnp.concatenate(right, axis=0),
            preferred_element_type=F32,
        )

    def share(stage, d):
        return remote(
            agg.at[stage, d], xsum.at[stage, d], sp, stage * NX + d, row, rep_x(d)
        )

    def summed_over_x(stage, h):
        def target(i, carry):
            d = (i + 1) % NX
            first = (h * NX + (x + d) % NX) * per_owner

            def one(j, inner):
                value = product(first + j)
                own[j] = value
                agg[stage, d, j] = value.astype(ROW_SUM)
                return inner

            lax.fori_loop(0, per_owner, one, 0)

            @pl.when(i < NX - 1)
            def _():
                share(stage, d).start()

            return carry

        lax.fori_loop(0, NX, target, 0)
        for d in range(1, NX):
            share(stage, d).wait_recv()
            pending.append(share(stage, d))
        out = own[...]
        for d in range(1, NX):
            out = out + xsum[stage, d].astype(F32)
        return out

    zsend[...] = summed_over_x(0, 1 - zh).astype(HALF_SUM)
    pl.semaphore_wait(far_sem, len(close))
    partner = z_dev(NZ)
    h_copy = remote(zsend, zsum, sh, 0, partner[0], partner[1])
    h_copy.start()
    kept = summed_over_x(1, zh)
    h_copy.wait_recv()
    pending.append(h_copy)
    summed = kept + zsum[...].astype(F32)
    aggregate = summed.reshape(own_rows, edge).astype(BF16)

    weight_copy.wait()
    preact = jnp.dot(aggregate, weight_ref[...], preferred_element_type=F32)
    sigmoid = jax.nn.sigmoid(preact)
    act_ref[...] = (preact * sigmoid).astype(BF16)
    slope = sigmoid * (1.0 + preact * (1.0 - sigmoid))
    cot_copy.wait()
    pre_grad = (cot[...].astype(F32) * slope).astype(BF16)
    part = lax.dot_general(
        aggregate, pre_grad, (((0,), (0,)), ((), ())), preferred_element_type=F32
    )
    tall, wide = wsend.shape[1:]
    across = part.shape[1] // wide
    for t in range(nq):
        top, left = (t // across) * tall, (t % across) * wide
        wsend[t] = part[top : top + tall, left : left + wide].astype(GRAD_A)

    w_copies = []
    for d in range(1, nq):
        copy = remote(wsend.at[q_at(d)], wrecv.at[q], sw, d, row_q(d), rep)
        copy.start()
        w_copies.append(copy)
    wrecv[q] = wsend[q]
    for copy in w_copies:
        copy.wait_recv()
    pending += w_copies
    xgrad[x] = functools.reduce(
        lambda a, b: a + b, [wrecv[t].astype(F32) for t in range(nq)]
    ).astype(GRAD_B)
    v_copies = []
    for d in range(1, NX):
        copy = remote(xgrad.at[x], xgrad.at[x], sv, d, row, rep_x(d))
        copy.start()
        v_copies.append(copy)
    for copy in v_copies:
        copy.wait_recv()
    pending += v_copies
    zgrad[z] = functools.reduce(
        lambda a, b: a + b, [xgrad[t].astype(F32) for t in range(NX)]
    ).astype(GRAD_B)
    u_copies = []
    for d in range(1, NZ * NH):
        r, p = z_dev(d)
        copy = remote(zgrad.at[z], zgrad.at[z], su, d, r, p)
        copy.start()
        u_copies.append(copy)
    for copy in u_copies:
        copy.wait_recv()
    pending += u_copies
    wfull[q] = functools.reduce(
        lambda a, b: a + b, [zgrad[t].astype(F32) for t in range(NZ * NH)]
    ).astype(GRAD_B)
    o_copies = []
    for d in range(1, nq):
        copy = remote(wfull.at[q], wfull.at[q], so, d, row_q(d), rep)
        copy.start()
        o_copies.append(copy)
    for copy in o_copies:
        copy.wait_recv()
    pending += o_copies
    for t in range(nq):
        top, left = (t // across) * tall, (t % across) * wide
        grad_ref[top : top + tall, left : left + wide] = wfull[t].astype(F32)

    for copy in pending:
        copy.wait_send()


def body(features, weight, section_source, tile_columns, tile_counts, tile_values, cotangent):
    rows, width = features.shape
    sections, blocks, slots, edge, _ = tile_values.shape
    hidden = weight.shape[1]
    nq = NY * NC
    piece = edge // NZ
    own_rows = rows // (NH * NX)
    per_owner = blocks // (NH * NX)
    per_x = NZ // NX
    tall = width * (hidden // edge) // nq
    dma = pltpu.SemaphoreType.DMA
    counts = [nq, 2 * NX, NX, NZ, NZ, NY, NY, NH * NX, 1, nq, NX, NZ * NH, nq]
    smem = pl.BlockSpec(memory_space=pltpu.SMEM)
    vmem = pl.BlockSpec(memory_space=pltpu.VMEM)
    hbm = pl.BlockSpec(memory_space=pltpu.HBM)
    return pl.pallas_call(
        kernel,
        out_shape=(
            jax.ShapeDtypeStruct((own_rows, hidden), BF16),
            jax.ShapeDtypeStruct((width, hidden), F32),
        ),
        in_specs=[smem, smem, smem, hbm, hbm, hbm, hbm],
        out_specs=(vmem, vmem),
        scratch_shapes=[
            pltpu.VMEM(tile_values.shape, BF16),
            pltpu.VMEM((own_rows, hidden), BF16),
            pltpu.VMEM(weight.shape, BF16),
            pltpu.VMEM((NH, NX, piece, width), BF16),
            pltpu.VMEM((nq, per_x, piece, width), BF16),
            pltpu.VMEM((NX, NH, sections, per_x, piece, width), BF16),
            pltpu.VMEM((NH, sections, NZ, piece, width), BF16),
            pltpu.VMEM((NZ, NH, sections, piece, width), BF16),
            pltpu.VMEM((NH, sections, piece, width), BF16),
            pltpu.VMEM((sections, blocks + 1, NZ, piece, width), BF16),
            pltpu.VMEM((NH, NX, per_owner, edge, width), ROW_SUM),
            pltpu.VMEM((NH, NX, per_owner, edge, width), ROW_SUM),
            pltpu.VMEM((per_owner, edge, width), F32),
            pltpu.VMEM((per_owner, edge, width), HALF_SUM),
            pltpu.VMEM((per_owner, edge, width), HALF_SUM),
            pltpu.VMEM((nq, tall, edge), GRAD_A),
            pltpu.VMEM((nq, tall, edge), GRAD_A),
            pltpu.VMEM((NX, tall, edge), GRAD_B),
            pltpu.VMEM((NZ * NH, tall, edge), GRAD_B),
            pltpu.VMEM((nq, tall, edge), GRAD_B),
            dma((4,)),
            pltpu.SemaphoreType.REGULAR,
        ]
        + [dma((n,)) for n in counts for _ in range(2)],
        compiler_params=pltpu.CompilerParams(
            collective_id=0, has_side_effects=True, vmem_limit_bytes=62 * 1024 * 1024
        ),
        cost_estimate=pl.CostEstimate(
            flops=2 * sections * blocks * slots * edge * edge * width,
            bytes_accessed=tile_values.size * 2,
            transcendentals=own_rows * hidden,
        ),
    )(
        section_source,
        tile_columns.transpose(2, 0, 1),
        tile_counts,
        weight,
        features.reshape(rows // piece, piece, width),
        tile_values,
        cotangent,
    )


def solution(mesh):
    in_specs = (
        P("row", None),
        P(),
        P("rep"),
        P("rep", "row", None),
        P("rep", "row"),
        P("rep", "row", None, None, None),
        P("row", None),
    )
    out_specs = (P(("row", "rep"), None), P())
    return jax.shard_map(body, mesh=mesh, in_specs=in_specs, out_specs=out_specs, check_vma=False)
```

time: 128 us -> 102 us (0.80)
  Pallas kernels: 118 us -> 97.8 us
  local copies, waits for them, and re-layouts: 8.41 us -> 3.14 us
    pallas_call x1, Pallas kernels: 118 us -> 97.8 us  [body(): pl.pallas_call(kernel, out_shape=(jax.ShapeDtypeStruct((own_rows, hidden)...]
    unnamed x15 -> x2, local copies, waits for them, and re-layouts: 8.41 us -> 3.14 us
where the time goes in v2:
time: 102 us
  Pallas kernels  97.8 us (96%)
  local copies, waits for them, and re-layouts  3.14 us (3%)
    pallas_call x1, Pallas kernels, body(): pl.pallas_call(kernel, out_shape=(jax.ShapeDtypeStruct((own_rows, hidden)...  97.8 us
    unnamed x2, local copies, waits for them, and re-layouts  3.14 us

profile of v2, /device:TPU:1, one launch (start us, length us, event | category | flops | bytes accessed | tf_op | source)
XLA Modules:
  0.0 101.6 jit_solution(6863245639879512670)
XLA Ops:
  0.6 97.8 %shard_map.86 = (bf16[256,256]{1,0:T(8,128)(2,1)}, f32[128,256]{1,0:T(8,128)}) custom-call(s32[2]{0:T(128)} %source_ref.1, s32[3,2,16]{2,1,0:T(2,128)} %bitcast.3, s32[2,16]{1,0:T(2,128)} %count_ref.1, bf16[128,256]{1,0:T(8,128)(2,1)} %weight_hbm.1, bf16[128,16,128]{2,1,0:T(8,128)(2,1)} %bitcast.2, bf16[2,16,3,128,128]{4,3,2,1,0:T(8,128)(2,1)} %tiles_ref.1, ...), custom_call_target="tpu_custom_call" | custom-call | flops 402653184 | bytes 3145728 | tf_op jit(solution)/shard_map/pallas_call | solution.py:426
  98.4 1.6 %copy.11 = bf16[256,256]{1,0:T(8,128)(2,1)} copy(bf16[256,256]{1,0:T(8,128)(2,1)} %get-tuple-element.4) | data formatting | bytes 262144
  100.0 1.6 %copy.12 = f32[128,256]{1,0:T(8,128)} copy(f32[128,256]{1,0:T(8,128)} %get-tuple-element.5) | data formatting | bytes 262144

commit v3 on v2

--- a/solution.py
+++ b/solution.py
@@ -78,6 +78,9 @@
         dy, dc = d // NC, d % NC
         return ((y + dy) % NY) * NC + (c + dc) % NC
 
+    q_far = sorted(range(1, nq), key=lambda d: -min(d // NC, NY - d // NC))
+    z_far = sorted(range(1, NZ * NH), key=lambda d: -min(d, NZ * NH - d))
+
     def row_q(d):
         return zl * nq + q_at(d)
 
@@ -92,16 +95,16 @@
         return (zz % NZ) * nq + q, (zz // NZ) * NX + x
 
     barrier = pltpu.get_barrier_semaphore()
-    peers = [(row_q(d), rep) for d in range(1, nq)]
+    peers = [(row_q(d), rep) for d in q_far]
     peers += [(row, rep_x(d)) for d in range(1, NX)]
     half = NZ // 2
-    close = [d for n in range(1, half + 1) for d in (-n, n)]
+    close = [d for n in range(half, 0, -1) for d in (-n, n)]
     peers += [z_dev(d) for d in close]
     over = (zl // half) * NZ - half
     over_row, over_rep = z_dev(over)
     over_h = over_rep // NX
     peers += [(over_row, over_h * NX + (x + d) % NX) for d in range(1, NX)]
-    for r, p in peers:
+    for r, p in reversed(peers):
         pl.semaphore_signal(
             barrier, inc=1, device_id={"row": r, "rep": p}, device_id_type=MESH
         )
@@ -148,7 +151,7 @@
     for copy in id_copies:
         copy.start()
     a_copies = []
-    for d in range(1, nq):
+    for d in q_far:
         copy = remote(rows_for(q_at(d)), cand.at[q], sa, d, row_q(d), rep)
         copy.start()
         a_copies.append(copy)
@@ -358,7 +361,7 @@
         wsend[t] = part[top : top + tall, left : left + wide].astype(GRAD_A)
 
     w_copies = []
-    for d in range(1, nq):
+    for d in q_far:
         copy = remote(wsend.at[q_at(d)], wrecv.at[q], sw, d, row_q(d), rep)
         copy.start()
         w_copies.append(copy)
@@ -381,7 +384,7 @@
         lambda a, b: a + b, [xgrad[t].astype(F32) for t in range(NX)]
     ).astype(GRAD_B)
     u_copies = []
-    for d in range(1, NZ * NH):
+    for d in z_far:
         r, p = z_dev(d)
         copy = remote(zgrad.at[z], zgrad.at[z], su, d, r, p)
         copy.start()
@@ -393,7 +396,7 @@
         lambda a, b: a + b, [zgrad[t].astype(F32) for t in range(NZ * NH)]
     ).astype(GRAD_B)
     o_copies = []
-    for d in range(1, nq):
+    for d in q_far:
         copy = remote(wfull.at[q], wfull.at[q], so, d, row_q(d), rep)
         copy.start()
         o_copies.append(copy)
@@ -426,8 +429,8 @@
     return pl.pallas_call(
         kernel,
         out_shape=(
-            jax.ShapeDtypeStruct((own_rows, hidden), BF16),
-            jax.ShapeDtypeStruct((width, hidden), F32),
+            pltpu.VMEM((own_rows, hidden), BF16),
+            pltpu.VMEM((width, hidden), F32),
         ),
         in_specs=[smem, smem, smem, hbm, hbm, hbm, hbm],
         out_specs=(vmem, vmem),

time: 102 us -> 98.4 us (0.965)
  local copies, waits for them, and re-layouts: 3.14 us -> 1.31 us
  Pallas kernels: 97.8 us -> 96.2 us
    unnamed x2, local copies, waits for them, and re-layouts: 3.14 us -> 1.31 us
    pallas_call x1, Pallas kernels: 97.8 us -> 96.2 us  [body(): pl.pallas_call(kernel, out_shape=(pltpu.VMEM((own_rows, hidden), BF16), p...]
where the time goes in v3:
time: 98.4 us; the launch traced here: 98.2 us
  Pallas kernels  96.2 us (98%)
  local copies, waits for them, and re-layouts  1.31 us (1%)
    pallas_call x1, Pallas kernels, body(): pl.pallas_call(kernel, out_shape=(pltpu.VMEM((own_rows, hidden), BF16), p...  96.2 us

profile of v3, /device:TPU:1, one launch (start us, length us, event | category | flops | bytes accessed | tf_op | source)
XLA Modules:
  0.0 98.2 jit_solution(13216844362099630828)
XLA Ops:
  0.6 96.2 %shard_map.86 = (bf16[256,256]{1,0:T(8,128)(2,1)S(1)}, f32[128,256]{1,0:T(8,128)S(1)}) custom-call(s32[2]{0:T(128)} %source_ref.1, s32[3,2,16]{2,1,0:T(2,128)} %bitcast.3, s32[2,16]{1,0:T(2,128)} %count_ref.1, bf16[128,256]{1,0:T(8,128)(2,1)} %weight_hbm.1, bf16[128,16,128]{2,1,0:T(8,128)(2,1)} %bitcast.2, bf16[2,16,3,128,128]{4,3,2,1,0:T(8,128)(2,1)} %tiles_ref.1, ...), custom_call_target="tpu_custom_call" | custom-call | flops 402653184 | bytes 3145728 | tf_op jit(solution)/shard_map/pallas_call | solution.py:429
  96.8 0.7 copy.11
  97.5 0.7 copy.12

commit v4 on v3

--- a/solution.py
+++ b/solution.py
@@ -87,6 +87,12 @@
     def rep_x(d):
         return zh * NX + (x + d) % NX
 
+    def x_order(i):
+        if NX != 4:
+            return (i + 1) % NX
+        late = i // 2
+        return late * (3 - i) + (1 - late) * (i + 2)
+
     def z_pos(d):
         return (z + d + NZ * NH) % (NZ * NH)
 
@@ -181,7 +187,7 @@
         )
 
     def choose(i, carry):
-        d = (i + 1) % NX
+        d = x_order(i)
         t = (x + d) % NX
         for h in range(NH):
             for k in range(section_count):
@@ -307,7 +313,7 @@
 
     def summed_over_x(stage, h):
         def target(i, carry):
-            d = (i + 1) % NX
+            d = x_order(i)
             first = (h * NX + (x + d) % NX) * per_owner
 
             def one(j, inner):
@@ -328,26 +334,33 @@
         for d in range(1, NX):
             share(stage, d).wait_recv()
             pending.append(share(stage, d))
-        out = own[...]
+
+    def total(stage, j):
+        out = own[j]
         for d in range(1, NX):
-            out = out + xsum[stage, d].astype(F32)
+            out = out + xsum[stage, d, j].astype(F32)
         return out
 
-    zsend[...] = summed_over_x(0, 1 - zh).astype(HALF_SUM)
+    summed_over_x(0, 1 - zh)
     pl.semaphore_wait(far_sem, len(close))
     partner = z_dev(NZ)
-    h_copy = remote(zsend, zsum, sh, 0, partner[0], partner[1])
-    h_copy.start()
-    kept = summed_over_x(1, zh)
-    h_copy.wait_recv()
-    pending.append(h_copy)
-    summed = kept + zsum[...].astype(F32)
+    h_copies = []
+    for j in range(per_owner):
+        zsend[j] = total(0, j).astype(HALF_SUM)
+        copy = remote(zsend.at[j], zsum.at[j], sh, j, partner[0], partner[1])
+        copy.start()
+        h_copies.append(copy)
+    summed_over_x(1, zh)
+    kept = [total(1, j) for j in range(per_owner)]
+    for copy in h_copies:
+        copy.wait_recv()
+    pending += h_copies
+    summed = jnp.stack([kept[j] + zsum[j].astype(F32) for j in range(per_owner)])
     aggregate = summed.reshape(own_rows, edge).astype(BF16)
 
     weight_copy.wait()
     preact = jnp.dot(aggregate, weight_ref[...], preferred_element_type=F32)
     sigmoid = jax.nn.sigmoid(preact)
-    act_ref[...] = (preact * sigmoid).astype(BF16)
     slope = sigmoid * (1.0 + preact * (1.0 - sigmoid))
     cot_copy.wait()
     pre_grad = (cot[...].astype(F32) * slope).astype(BF16)
@@ -365,6 +378,7 @@
         copy = remote(wsend.at[q_at(d)], wrecv.at[q], sw, d, row_q(d), rep)
         copy.start()
         w_copies.append(copy)
+    act_ref[...] = (preact * sigmoid).astype(BF16)
     wrecv[q] = wsend[q]
     for copy in w_copies:
         copy.wait_recv()
@@ -422,7 +436,7 @@
     per_x = NZ // NX
     tall = width * (hidden // edge) // nq
     dma = pltpu.SemaphoreType.DMA
-    counts = [nq, 2 * NX, NX, NZ, NZ, NY, NY, NH * NX, 1, nq, NX, NZ * NH, nq]
+    counts = [nq, 2 * NX, NX, NZ, NZ, NY, NY, NH * NX, per_owner, nq, NX, NZ * NH, nq]
     smem = pl.BlockSpec(memory_space=pltpu.SMEM)
     vmem = pl.BlockSpec(memory_space=pltpu.VMEM)
     hbm = pl.BlockSpec(memory_space=pltpu.HBM)

time: 98.4 us -> 97.2 us (0.988)
  Pallas kernels: 96.2 us -> 95.1 us
    pallas_call x1, Pallas kernels: 96.2 us -> 95.1 us  [body(): pl.pallas_call(kernel, out_shape=(pltpu.VMEM((own_rows, hidden), BF16), p...]
where the time goes in v4:
time: 97.2 us; the launch traced here: 97 us
  Pallas kernels  95.1 us (98%)
  local copies, waits for them, and re-layouts  1.31 us (1%)
    pallas_call x1, Pallas kernels, body(): pl.pallas_call(kernel, out_shape=(pltpu.VMEM((own_rows, hidden), BF16), p...  95.1 us

profile of v4, /device:TPU:1, one launch (start us, length us, event | category | flops | bytes accessed | tf_op | source)
XLA Modules:
  0.0 97.0 jit_solution(3867158974295668158)
XLA Ops:
  0.6 95.1 %shard_map.86 = (bf16[256,256]{1,0:T(8,128)(2,1)S(1)}, f32[128,256]{1,0:T(8,128)S(1)}) custom-call(s32[2]{0:T(128)} %source_ref.1, s32[3,2,16]{2,1,0:T(2,128)} %bitcast.3, s32[2,16]{1,0:T(2,128)} %count_ref.1, bf16[128,256]{1,0:T(8,128)(2,1)} %weight_hbm.1, bf16[128,16,128]{2,1,0:T(8,128)(2,1)} %bitcast.2, bf16[2,16,3,128,128]{4,3,2,1,0:T(8,128)(2,1)} %tiles_ref.1, ...), custom_call_target="tpu_custom_call" | custom-call | flops 402653184 | bytes 3145728 | tf_op jit(solution)/shard_map/pallas_call | solution.py:443
  95.7 0.7 copy.11
  96.4 0.7 copy.12
